TPU v7x, 32 devices: a whole 2x2x4 slice. The times are simulated.
32 devices in a mesh: pipe: 2 (over core), obs: 4 (over y, x), patch: 4 (over z).
Axes of the slice: x: 2, y: 2, z: 4, core: 2. Of those that a mesh axis runs over, the one named last changes fastest.
Arguments:
- patch_tokens: bfloat16 [2048, 2048], P('patch', 'obs'), may hold values from -40 to 40
- obs_tokens: bfloat16 [1024, 2048], P('patch', 'obs'), may hold values from -40 to 40
- footprint: int32 [16, 4], P('patch'), may hold values from 0 to 7, as said below
- list_counts: int32 [16], P('patch'), may hold values from 1 to 4
- footprint_bias: float32 [16, 4], P('patch'), may hold values from -4 to 290
- w_query: bfloat16 [2, 2048, 2048], P('pipe', None, 'obs'), may hold values from -0.125 to 0.125
- w_key: bfloat16 [2, 2048, 2048], P('pipe', None, 'obs'), may hold values from -0.125 to 0.125
- w_value: bfloat16 [2, 2048, 2048], P('pipe', None, 'obs'), may hold values from -0.125 to 0.125
- w_out: bfloat16 [2, 2048, 2048], P('pipe', 'obs'), may hold values from -0.125 to 0.125
- patch_gain: float32 [2, 2048], P('pipe'), may hold values from 0.1 to 1.9
- obs_gain: float32 [2, 2048], P('pipe'), may hold values from 0.1 to 1.9
Outputs:
- sections: bfloat16 [2, 2048, 2048], P('pipe', 'patch', 'obs')
Inputs may be any that keep to these rules, and one draw needn't show every extreme that they name: `footprint`: entries are global observation block indices. In each row the first list_counts entries (the live ones) are distinct, the rest are to be ignored. For a device along patch and any device along patch, all live entries of the first device's rows that lie in the second device's range of 2 blocks name one and the same block.
All inputs are finite; a program needn't handle non-finite values.
Results may differ from a plain program's by a relative error of at most 0.012.
Values may be sent and summed in bfloat16 or wider, within the bound.
A program may use at most 64 MiB of HBM per device.

v0:
```python
import jax
import jax.numpy as jnp
from jax import lax
from jax.sharding import PartitionSpec as P

HS = 128
BLK = 128
MB = 128


def passed_along(value, axis, steps):
    count = lax.axis_size(axis)
    first, last = (max(0, -steps), min(count, count - steps))
    return lax.ppermute(value, axis, [(source, source + steps) for source in range(first, last)])


def rms_round(values, gain):
    widened = values.astype(jnp.float32)
    scaled = widened * lax.rsqrt(jnp.mean(widened * widened, axis=-1, keepdims=True) + 1e-05)
    return (scaled * gain).astype(jnp.bfloat16)


def store_rows(sections, out_piece, is_valid, row_start):
    current = lax.dynamic_slice_in_dim(sections, row_start, out_piece.shape[0], 1)
    kept = jnp.where(is_valid, out_piece[None], current)
    return lax.dynamic_update_slice_in_dim(sections, kept, row_start, 1)


def on_device(
    patch_tokens,
    obs_tokens,
    footprint,
    list_counts,
    footprint_bias,
    w_query,
    w_key,
    w_value,
    w_out,
    patch_gain,
    obs_gain,
):
    pipe_segment = lax.axis_index("pipe")
    segment_count = lax.axis_size("pipe")
    obs_column = lax.axis_index("obs")
    feature_part = patch_tokens.shape[1]
    full_features = feature_part * lax.axis_size("obs")
    head_width = w_query.shape[2]
    heads_here = head_width // HS
    list_slots = footprint.shape[1]
    micro_count = patch_tokens.shape[0] // MB
    blocks_micro = MB // BLK
    score_scale = HS ** (-0.5)
    observed = lax.all_gather(obs_tokens, "obs", axis=1, tiled=True)
    obs_normed = rms_round(observed, obs_gain[0])
    key_values = jnp.concatenate(
        [
            jnp.dot(obs_normed, w_key[0], preferred_element_type=jnp.float32).astype(jnp.bfloat16),
            jnp.dot(obs_normed, w_value[0], preferred_element_type=jnp.float32).astype(
                jnp.bfloat16
            ),
        ],
        axis=1,
    )
    local_blocks = key_values.reshape(-1, BLK, 2 * head_width)
    kv_table = lax.all_gather(local_blocks, "patch", axis=0, tiled=True)

    def attend_block(segment_input, micro_index):
        patch_normed = rms_round(segment_input, patch_gain[0])
        queries = (
            jnp.dot(patch_normed, w_query[0], preferred_element_type=jnp.float32) * score_scale
        ).astype(jnp.bfloat16)
        queries = queries.reshape(blocks_micro, BLK, heads_here, HS)
        first_block = micro_index * blocks_micro
        slot_part = lax.dynamic_slice_in_dim(footprint, first_block, blocks_micro, 0)
        count_part = lax.dynamic_slice_in_dim(list_counts, first_block, blocks_micro, 0)
        bias_part = lax.dynamic_slice_in_dim(footprint_bias, first_block, blocks_micro, 0)
        picked = kv_table[slot_part].reshape(blocks_micro, list_slots * BLK, 2 * head_width)
        key_part = picked[:, :, :head_width].reshape(blocks_micro, list_slots * BLK, heads_here, HS)
        value_part = picked[:, :, head_width:].reshape(
            blocks_micro, list_slots * BLK, heads_here, HS
        )
        scores = jnp.einsum(
            "bqhd,bkhd->bhqk", queries, key_part, preferred_element_type=jnp.float32
        )
        alive_mask = jnp.repeat(jnp.arange(list_slots)[None, :] < count_part[:, None], BLK, axis=1)
        added = jnp.repeat(bias_part, BLK, axis=1)
        scores = jnp.where(alive_mask[:, None, None, :], scores + added[:, None, None, :], -1e30)
        row_max = jnp.max(scores, axis=-1, keepdims=True)
        weights = jnp.exp(scores - row_max)
        weights = (weights / jnp.sum(weights, axis=-1, keepdims=True)).astype(jnp.bfloat16)
        context = jnp.einsum(
            "bhqk,bkhd->bqhd", weights, value_part, preferred_element_type=jnp.float32
        ).astype(jnp.bfloat16)
        context = context.reshape(MB, head_width)
        return jnp.dot(context, w_out[0], preferred_element_type=jnp.float32)

    def spare_block(segment_input, micro_index):
        return jnp.zeros((MB, full_features), jnp.float32)

    tick_total = micro_count + segment_count - 1
    sections = jnp.zeros((1, patch_tokens.shape[0], feature_part), jnp.bfloat16)
    rows_all = lax.all_gather(patch_tokens, "obs", axis=1, tiled=True)
    arriving = jnp.zeros((MB, full_features), jnp.bfloat16)
    for tick_num in range(tick_total):
        tick_micro = tick_num - pipe_segment
        is_valid = (tick_micro >= 0) & (tick_micro < micro_count)
        micro_index = jnp.clip(tick_micro, 0, micro_count - 1)
        own_rows = lax.dynamic_slice_in_dim(rows_all, micro_index * MB, MB, 0)
        segment_input = jnp.where(pipe_segment == 0, own_rows, arriving)
        partial_value = lax.cond(is_valid, attend_block, spare_block, segment_input, micro_index)
        head_total = lax.psum(partial_value.astype(jnp.bfloat16), "obs").astype(jnp.float32)
        segment_output = (segment_input.astype(jnp.float32) + head_total).astype(jnp.bfloat16)
        out_piece = lax.dynamic_slice_in_dim(
            segment_output, obs_column * feature_part, feature_part, 1
        )
        sections = store_rows(sections, out_piece, is_valid, micro_index * MB)
        if tick_num + 1 < tick_total:
            arriving = passed_along(segment_output, "pipe", 1)
    return sections


def solution(mesh):
    in_specs = (
        P("patch", "obs"),
        P("patch", "obs"),
        P("patch", None),
        P("patch"),
        P("patch", None),
        P("pipe", None, "obs"),
        P("pipe", None, "obs"),
        P("pipe", None, "obs"),
        P("pipe", "obs", None),
        P("pipe", None),
        P("pipe", None),
    )
    out_specs = P("pipe", "patch", "obs")
    return jax.shard_map(
        on_device, mesh=mesh, in_specs=in_specs, out_specs=out_specs, check_vma=False
    )
```

profile of v0, /device:TPU:1, one launch (start us, length us, event | category | flops | bytes accessed | tf_op | source)
XLA Modules:
  0.0 472.0 jit_solution(3355118318211876162)
XLA Ops:
  8.1 29.7 %all-gather.6.cloned.1.call-done = bf16[256,2048]{1,0:T(8,128)(2,1)} async-done(((bf16[256,512]{1,0:T(8,128)(2,1)}), bf16[256,2048]{1,0:T(8,128)(2,1)}) %all-gather.6.cloned.1.call-update) | async-done | bytes 1048592 | tf_op jit(solution)/shard_map/all_gather | solution.py:53
  43.3 31.5 %all-gather.4.cloned.1.call-done = bf16[512,2048]{1,0:T(8,128)(2,1)} async-done(((bf16[512,512]{1,0:T(8,128)(2,1)}), bf16[512,2048]{1,0:T(8,128)(2,1)}) %all-gather.4.cloned.1.call-update) | async-done | bytes 2097168 | tf_op jit(solution)/shard_map/all_gather | solution.py:102
  76.8 45.6 %all-gather.8.cloned.1.call-done = bf16[8,128,1024]{2,1,0:T(8,128)(2,1)} async-done(((bf16[2,128,1024]{2,1,0:T(8,128)(2,1)}), bf16[8,128,1024]{2,1,0:T(8,128)(2,1)}) %all-gather.8.cloned.1.call-update) | async-done | bytes 2097168 | tf_op jit(solution)/shard_map/all_gather | solution.py:65
  123.3 60.8 %all-reduce.6.cloned.1.call-done = bf16[128,2048]{1,0:T(8,128)(2,1)} async-done(((bf16[128,2048]{1,0:T(8,128)(2,1)}), bf16[128,2048]{1,0:T(8,128)(2,1)}) %all-reduce.6.cloned.1.call-update) | async-done | bytes 524304 | tf_op jit(solution)/shard_map/psum | solution.py:111
  186.8 2.5 collective-permute-done
  190.4 18.0 %conditional.6 = (bf16[128,2048]{1,0:T(8,128)(2,1)S(1)}) conditional(s32[]{:T(128)} %convert_element_type.207, () %tuple.37, (s32[]{:T(128)}, s32[4,4]{1,0:T(4,128)S(1)}, bf16[8,128,1024]{2,1,0:T(8,128)(2,1)}, s32[4]{0:T(128)S(1)}, bf16[128,2048]{1,0:T(8,128)(2,1)S(1)}, /*index=5*/f32[1,2048]{1,0:T(1,128)S(1)}, bf16[1,2048,512]{2,1,0:T(8,128)(2,1)}, ...), branch_computations={%region_7.8_spmd, %region_8.12_spmd} | conditional | flops 742591104 | bytes 16410298 | solution.py:110
  190.5 3.2 gather_fusion.1
  203.6 2.8 convolution_convert_fusion.1
  209.4 44.8 %all-reduce.8.cloned.1.call-done = bf16[128,2048]{1,0:T(8,128)(2,1)} async-done(((bf16[128,2048]{1,0:T(8,128)(2,1)}), bf16[128,2048]{1,0:T(8,128)(2,1)}) %all-reduce.8.cloned.1.call-update) | async-done | bytes 524304 | tf_op jit(solution)/shard_map/psum | solution.py:111
  256.6 2.6 collective-permute-done.1
  260.6 17.8 %conditional.7 = (bf16[128,2048]{1,0:T(8,128)(2,1)S(1)}) conditional(s32[]{:T(128)} %convert_element_type.212, () %tuple.39, (s32[]{:T(128)}, s32[4,4]{1,0:T(4,128)S(1)}, bf16[8,128,1024]{2,1,0:T(8,128)(2,1)}, s32[4]{0:T(128)S(1)}, bf16[128,2048]{1,0:T(8,128)(2,1)S(1)}, /*index=5*/f32[1,2048]{1,0:T(1,128)S(1)}, bf16[1,2048,512]{2,1,0:T(8,128)(2,1)}, ...), branch_computations={%region_13.14_spmd, %region_14.18_spmd} | conditional | flops 742591104 | bytes 16410298 | solution.py:110
  260.6 3.2 gather_fusion.2
  273.5 2.8 convolution_convert_fusion.2
  279.5 44.5 %all-reduce.10.cloned.1.call-done = bf16[128,2048]{1,0:T(8,128)(2,1)} async-done(((bf16[128,2048]{1,0:T(8,128)(2,1)}), bf16[128,2048]{1,0:T(8,128)(2,1)}) %all-reduce.10.cloned.1.call-update) | async-done | bytes 524304 | tf_op jit(solution)/shard_map/psum | solution.py:111
  326.5 2.6 collective-permute-done.2
  330.5 18.0 %conditional.8 = (bf16[128,2048]{1,0:T(8,128)(2,1)S(1)}) conditional(s32[]{:T(128)} %convert_element_type.217, () %tuple.41, (s32[]{:T(128)}, s32[4,4]{1,0:T(4,128)S(1)}, bf16[8,128,1024]{2,1,0:T(8,128)(2,1)}, s32[4]{0:T(128)S(1)}, bf16[128,2048]{1,0:T(8,128)(2,1)S(1)}, /*index=5*/f32[1,2048]{1,0:T(1,128)S(1)}, bf16[1,2048,512]{2,1,0:T(8,128)(2,1)}, ...), branch_computations={%region_19.20_spmd, %region_20.24_spmd} | conditional | flops 742591104 | bytes 16410298 | solution.py:110
  330.5 3.2 gather_fusion.3
  343.6 2.8 convolution_convert_fusion.3
  349.4 44.7 %all-reduce.12.cloned.1.call-done = bf16[128,2048]{1,0:T(8,128)(2,1)} async-done(((bf16[128,2048]{1,0:T(8,128)(2,1)}), bf16[128,2048]{1,0:T(8,128)(2,1)}) %all-reduce.12.cloned.1.call-update) | async-done | bytes 524304 | tf_op jit(solution)/shard_map/psum | solution.py:111
  396.6 2.5 collective-permute-done.3
  401.1 16.8 %conditional.9 = (bf16[128,2048]{1,0:T(8,128)(2,1)S(1)}) conditional(s32[]{:T(128)} %convert_element_type.222, () %tuple.43, (s32[]{:T(128)}, s32[4,4]{1,0:T(4,128)S(1)}, bf16[8,128,1024]{2,1,0:T(8,128)(2,1)}, s32[4]{0:T(128)S(1)}, bf16[128,2048]{1,0:T(8,128)(2,1)}, /*index=5*/f32[1,2048]{1,0:T(1,128)S(1)}, bf16[1,2048,512]{2,1,0:T(8,128)(2,1)}, ...), branch_computations={%region_25.26_spmd, %region_26.30_spmd} | conditional | flops 742591104 | bytes 20604658 | solution.py:110
  401.1 2.2 gather_fusion.4
  413.1 2.6 convolution_convert_fusion.4
  422.5 40.9 %all-reduce.14.cloned.1.call-done = bf16[128,2048]{1,0:T(8,128)(2,1)} async-done(((bf16[128,2048]{1,0:T(8,128)(2,1)}), bf16[128,2048]{1,0:T(8,128)(2,1)}) %all-reduce.14.cloned.1.call-update) | async-done | bytes 524304 | tf_op jit(solution)/shard_map/psum | solution.py:111
  (146 shorter events, 82.5 us)
Async XLA Ops:
  6.5 32.8 %copy-start = (bf16[1,2048,512]{2,1,0:T(8,128)(2,1)S(1)}, bf16[1,2048,512]{2,1,0:T(8,128)(2,1)}, u32[]{:S(2)}) copy-start(bf16[1,2048,512]{2,1,0:T(8,128)(2,1)} %param.28) | copy-start | bytes 6291460
  6.5 31.3 %all-gather.6.cloned.1.call-start = ((), (), s32[]{:S(2)}) async-start(), calls=%async_computation.1 | async-start | bytes 1310720 | tf_op jit(solution)/shard_map/all_gather | solution.py:53
  7.3 67.6 %all-gather.4.cloned.1.call-start = ((), (), s32[]{:S(2)}) async-start(), calls=%async_computation | async-start | bytes 2621440 | tf_op jit(solution)/shard_map/all_gather | solution.py:102
  8.0 114.3 %all-gather.8.cloned.1.call-start = ((), (), s32[]{:S(2)}) async-start(), calls=%async_computation.2 | async-start | bytes 2621440 | tf_op jit(solution)/shard_map/all_gather | solution.py:65
  39.3 2.2 copy-start.16
  39.3 2.2 copy-start.17
  42.3 80.0 %copy-start.18 = (f32[1,2048]{1,0:T(1,128)S(1)}, f32[1,2048]{1,0:T(1,128)}, u32[]{:S(2)}) copy-start(f32[1,2048]{1,0:T(1,128)} %param.30) | copy-start | bytes 24580
  42.4 80.0 %copy-start.19 = (s32[4,4]{1,0:T(4,128)S(1)}, s32[4,4]{1,0:T(4,128)}, u32[]{:S(2)}) copy-start(s32[4,4]{1,0:T(4,128)} %param.23) | copy-start | bytes 196
  42.4 80.0 %copy-start.20 = (f32[4,4]{1,0:T(4,128)S(1)}, f32[4,4]{1,0:T(4,128)}, u32[]{:S(2)}) copy-start(f32[4,4]{1,0:T(4,128)} %param.25) | copy-start | bytes 196
  42.4 80.0 %copy-start.21 = (s32[4]{0:T(128)S(1)}, s32[4]{0:T(128)}, u32[]{:S(2)}) copy-start(s32[4]{0:T(128)} %param.24) | copy-start | bytes 52
  43.3 140.8 %all-reduce.6.cloned.1.call-start = ((), (), s32[]{:S(2)}) async-start(), calls=%async_computation.3 | async-start | bytes 1048576 | tf_op jit(solution)/shard_map/psum | solution.py:111
  123.3 130.8 %all-reduce.8.cloned.1.call-start = ((), (), s32[]{:S(2)}) async-start(), calls=%async_computation.4 | async-start | bytes 1048576 | tf_op jit(solution)/shard_map/psum | solution.py:111
  185.5 3.8 collective-permute-start
  209.3 114.7 %all-reduce.10.cloned.1.call-start = ((), (), s32[]{:S(2)}) async-start(), calls=%async_computation.5 | async-start | bytes 1048576 | tf_op jit(solution)/shard_map/psum | solution.py:111
  255.3 5.3 %copy-start.10 = (bf16[128,2048]{1,0:T(8,128)(2,1)}, bf16[128,2048]{1,0:T(8,128)(2,1)S(1)}, u32[]{:S(2)}) copy-start(bf16[128,2048]{1,0:T(8,128)(2,1)S(1)} %add_convert_fusion.2) | copy-start | bytes 1572868
  255.3 3.9 collective-permute-start.1
  279.2 114.9 %all-reduce.12.cloned.1.call-start = ((), (), s32[]{:S(2)}) async-start(), calls=%async_computation.6 | async-start | bytes 1048576 | tf_op jit(solution)/shard_map/psum | solution.py:111
  325.2 5.3 %copy-start.11 = (bf16[128,2048]{1,0:T(8,128)(2,1)}, bf16[128,2048]{1,0:T(8,128)(2,1)S(1)}, u32[]{:S(2)}) copy-start(bf16[128,2048]{1,0:T(8,128)(2,1)S(1)} %add_convert_fusion.1) | copy-start | bytes 1572868
  325.2 3.9 collective-permute-start.2
  349.3 114.1 %all-reduce.14.cloned.1.call-start = ((), (), s32[]{:S(2)}) async-start(), calls=%async_computation.7 | async-start | bytes 1048576 | tf_op jit(solution)/shard_map/psum | solution.py:111
  395.3 5.8 %copy-start.12 = (bf16[128,2048]{1,0:T(8,128)(2,1)}, bf16[128,2048]{1,0:T(8,128)(2,1)S(1)}, u32[]{:S(2)}) copy-start(bf16[128,2048]{1,0:T(8,128)(2,1)S(1)} %add_convert_fusion) | copy-start | bytes 1572868
  395.3 3.8 collective-permute-start.3
  404.4 4.7 copy-start.1
  422.5 40.9 %copy-start.3 = (bf16[1,512,512]{2,1,0:T(8,128)(2,1)}, bf16[1,512,512]{2,1,0:T(8,128)(2,1)S(1)}, u32[]{:S(2)}) copy-start(bf16[1,512,512]{2,1,0:T(8,128)(2,1)S(1)} %fusion.168) | copy-start | bytes 1572868
  (8 other events, 9.3 us)
Sparse Core Ops, SparseCore 0:
  9.2 28.5 all-gather.5
  39.6 35.1 all-gather.3
  76.4 45.9 all-gather.7
  125.2 58.8 all-reduce.5
  209.4 44.6 all-reduce.7
  279.4 44.6 all-reduce.9
  349.5 44.6 all-reduce.11
  418.8 44.6 all-reduce.13
where the time goes:
time: 474 us; the launch traced here: 472 us
  waiting for transfers between devices  354 us (75%)
  matrix products  37.5 us (8%)
  local copies, waits for them, and re-layouts  36.6 us (8%)
  other arithmetic  23.9 us (5%)
  between operations  13.9 us (3%)
  starting transfers between devices  5.63 us (1%)
    psum x5, waiting for transfers between devices, on_device(): lax.psum(partial_value.astype(jnp.bfloat16), 'obs').astype(jnp.float32)  236 us
    all_gather x1, waiting for transfers between devices, on_device(): kv_table = lax.all_gather(local_blocks, 'patch', axis=0, tiled=True)  45.6 us
    all_gather x1, waiting for transfers between devices, on_device(): rows_all = lax.all_gather(patch_tokens, 'obs', axis=1, tiled=True)  31.5 us
    all_gather x1, waiting for transfers between devices, on_device(): observed = lax.all_gather(obs_tokens, 'obs', axis=1, tiled=True)  29.7 us
    gather x4, local copies, waits for them, and re-layouts, attend_block(): kv_table[slot_part].reshape(blocks_micro, list_slots * BLK, 2 * head_width)  11.7 us
    dot_general x4, matrix products, attend_block(): jnp.einsum('bhqk,bkhd->bqhd', weights, value_part, preferred_element_type...  11 us
    ppermute x4, waiting for transfers between devices, passed_along(): lax.ppermute(value, axis, [(source, source + steps) for source in range(f...  10.2 us
    cond x12, local copies, waits for them, and re-layouts  10.2 us
  transfers between devices with their start and end apart: 12, of which 12 were waited for; matrix products, arithmetic and copies ran while one was open for 2% of the time, Pallas kernels for 0%

commit v1 on v0

v1 whole, which is shorter than its diff:
```python
import functools
import jax
import jax.numpy as jnp
from jax import lax
from jax.experimental import pallas as pl
from jax.experimental.pallas import tpu as pltpu
from jax.sharding import PartitionSpec as P

HS = 128
BLK = 128
HALF = BLK // 2
EPS = 1e-05
NEG = -1e30
F32 = jnp.float32
BF16 = jnp.bfloat16


def rms_round(values, gain):
    widened = values.astype(F32)
    scaled = widened * lax.rsqrt(jnp.mean(widened * widened, axis=-1, keepdims=True) + EPS)
    return (scaled * gain).astype(BF16)


def remote(src, dst, send_sem, recv_sem, pipe, obs, patch):
    return pltpu.make_async_remote_copy(
        src_ref=src,
        dst_ref=dst,
        send_sem=send_sem,
        recv_sem=recv_sem,
        device_id={"pipe": pipe, "obs": obs, "patch": patch},
        device_id_type=pl.DeviceIdType.MESH,
    )


def kernel(
    n_obs,
    n_patch,
    patch_hbm,
    obs_hbm,
    footprint,
    counts,
    slot_bias,
    wq_hbm,
    wk_hbm,
    wv_hbm,
    wo_hbm,
    patch_gain,
    obs_gain,
    out,
    wq,
    wk,
    wv,
    wo,
    xbuf,
    zbuf,
    sel,
    ofull,
    keys,
    vals,
    queries,
    context,
    pbuf,
    rbuf,
    x1,
    bias,
    w_sem,
    own_sem,
    z_send,
    z_recv,
    o_send,
    o_recv,
    f_send,
    x_send,
    x_recv,
    r_send,
    r_recv,
):
    p = lax.axis_index("pipe")
    o = lax.axis_index("obs")
    z = lax.axis_index("patch")
    rows_total, feat = out.shape
    micro = rows_total // BLK
    heads = wq.shape[1] // HS
    range_blocks = zbuf.shape[1]
    half_rows = sel.shape[0]
    peers = [lax.rem(o + k, n_obs) for k in range(n_obs)]
    zpeers = [lax.rem(z + k, n_patch) for k in range(n_patch)]

    def cols(index):
        return pl.ds(pl.multiple_of(index * feat, feat), feat)

    def rows(index):
        return pl.ds(pl.multiple_of(index * BLK, BLK), BLK)

    barrier = pltpu.get_barrier_semaphore()
    for k in range(n_obs):
        pl.semaphore_signal(
            barrier, inc=1, device_id={"pipe": 1 - p, "obs": peers[k], "patch": z},
            device_id_type=pl.DeviceIdType.MESH,
        )
        if k:
            pl.semaphore_signal(
                barrier, inc=1, device_id={"pipe": p, "obs": peers[k], "patch": z},
                device_id_type=pl.DeviceIdType.MESH,
            )
    for k in range(1, n_patch):
        pl.semaphore_signal(
            barrier, inc=1, device_id={"pipe": p, "obs": o, "patch": zpeers[k]},
            device_id_type=pl.DeviceIdType.MESH,
        )
    own_obs = pltpu.make_async_copy(obs_hbm.at[:, p], zbuf.at[z], own_sem.at[0])
    own_obs.start()
    own_patch = pltpu.make_async_copy(patch_hbm, xbuf.at[:, cols(o)], own_sem.at[1])

    @pl.when(p == 0)
    def _():
        own_patch.start()

    w_copies = [
        pltpu.make_async_copy(src, dst, w_sem.at[i])
        for i, (src, dst) in enumerate(
            ((wq_hbm, wq), (wk_hbm, wk), (wv_hbm, wv), (wo_hbm, wo))
        )
    ]
    for copy in w_copies:
        copy.start()
    pl.semaphore_wait(barrier, 2 * n_obs - 1 + n_patch - 1)

    def z_copy(k):
        return remote(
            obs_hbm.at[:, p], zbuf.at[z], z_send.at[k], z_recv.at[z], p, o, zpeers[k]
        )

    def patch_copy(m, k):
        return remote(
            patch_hbm.at[rows(m), :], xbuf.at[rows(m), cols(o)],
            x_send.at[m, k], x_recv.at[m, o], 0, peers[k], z,
        )

    for k in range(1, n_patch):
        z_copy(k).start()

    @pl.when(p == 0)
    def _():
        @pl.loop(0, micro)
        def _(m):
            for k in range(1, n_obs):
                patch_copy(m, k).start()

    listed = footprint[...].astype(F32)
    slots = lax.broadcasted_iota(jnp.int32, listed.shape, 1)
    alive = slots < counts[...]
    added = slot_bias[...]
    col = lax.broadcasted_iota(jnp.int32, bias.shape, 1)
    source = lax.rem(lax.div(col, HALF), n_patch)
    full_bias = jnp.full(bias.shape, NEG, F32)
    wanted = []
    for zz in range(n_patch):
        low = zz * range_blocks
        match = alive & (listed >= float(low)) & (listed < float(low + range_blocks))
        one = jnp.max(jnp.where(match, added, NEG), axis=1, keepdims=True)
        full_bias = jnp.where(source == zz, one, full_bias)
        which = jnp.max(jnp.where(match, listed - float(low), 0.0), axis=1, keepdims=True)
        wanted.append(jnp.max(which, axis=0, keepdims=True))
    bias[...] = full_bias

    own_obs.wait()
    for k in range(1, n_patch):
        remote(
            obs_hbm.at[:, p], zbuf.at[zpeers[k]], z_send.at[k], z_recv.at[zpeers[k]],
            p, o, zpeers[k],
        ).wait_recv()
    for zz in range(n_patch):
        picked = zbuf[zz, 0].astype(F32)
        which = jnp.broadcast_to(wanted[zz], picked.shape)
        for k in range(1, range_blocks):
            picked = jnp.where(which == float(k), zbuf[zz, k].astype(F32), picked)
        sel[zz * HALF : (zz + 1) * HALF, :] = picked.astype(BF16)

    def sel_copy(k):
        if k == 0:
            return remote(
                sel, ofull.at[p, :, cols(o)], o_send.at[0], o_recv.at[p, o], 1 - p, o, z
            )
        return remote(
            sel, ofull.at[p, :, cols(o)], o_send.at[k], o_recv.at[p, o], p, peers[k], z
        )

    def forward(k):
        slab = ofull.at[p, :, cols(peers[k])]
        return remote(
            slab, slab, f_send.at[k], o_recv.at[p, peers[k]], 1 - p, o, z
        )

    for k in range(1, n_obs):
        sel_copy(k).start()
    sel_copy(0).start()
    own_sel = pltpu.make_async_copy(sel, ofull.at[p, :, cols(o)], own_sem.at[2])
    own_sel.start()

    w_copies[0].wait()
    score_scale = HS ** (-0.5)

    def project(m):
        for k in range(1, n_obs):
            remote(
                patch_hbm.at[rows(m), :], xbuf.at[rows(m), cols(peers[k])],
                x_send.at[m, k], x_recv.at[m, peers[k]], 0, peers[k], z,
            ).wait_recv()
        normed = rms_round(xbuf[rows(m), :], patch_gain[...])
        queries[rows(m), :] = (
            jnp.dot(normed, wq[...], preferred_element_type=F32) * score_scale
        ).astype(BF16)

    @pl.when(p == 0)
    def _():
        own_patch.wait()

        @pl.loop(0, micro)
        def _(m):
            project(m)

    for k in range(1, n_obs):
        slab = ofull.at[p, :, cols(peers[k])]
        remote(sel, slab, o_send.at[k], o_recv.at[p, peers[k]], p, peers[k], z).wait_recv()
        forward(k).start()
    own_sel.wait()
    for k in range(n_obs):
        slab = ofull.at[1 - p, :, cols(peers[k])]
        remote(
            slab, slab, f_send.at[k], o_recv.at[1 - p, peers[k]], 1 - p, o, z
        ).wait_recv()

    w_copies[1].wait()
    w_copies[2].wait()

    @pl.loop(0, 2)
    def _(h):
        normed = rms_round(ofull[h], obs_gain[...])
        here = pl.ds(pl.multiple_of(h * half_rows, half_rows), half_rows)
        keys[here, :] = jnp.dot(normed, wk[...], preferred_element_type=F32).astype(BF16)
        vals[here, :] = jnp.dot(normed, wv[...], preferred_element_type=F32).astype(BF16)

    w_copies[3].wait()

    def piece_copy(m, k):
        return remote(
            pbuf.at[peers[k], rows(m), :], rbuf.at[o, rows(m), :],
            r_send.at[m, k], r_recv.at[m, o], p, peers[k], z,
        )

    def x1_copy(m, k):
        return remote(
            x1.at[rows(m), :], xbuf.at[rows(m), cols(o)],
            x_send.at[micro + m, k], x_recv.at[m, o], 1, peers[k], z,
        )

    def attend(m):
        row_bias = bias[pl.ds(m, 1), :]
        for h in range(heads):
            head = slice(h * HS, (h + 1) * HS)
            scores = lax.dot_general(
                queries[rows(m), head], keys[:, head], (((1,), (1,)), ((), ())),
                preferred_element_type=F32,
            )
            scores = scores + row_bias
            weights = jnp.exp(scores - jnp.max(scores, axis=-1, keepdims=True))
            total = jnp.sum(weights, axis=-1, keepdims=True)
            mixed = jnp.dot(weights.astype(BF16), vals[:, head], preferred_element_type=F32)
            context[:, head] = (mixed / total).astype(BF16)
        for k in list(range(1, n_obs)) + [0]:
            pbuf[peers[k], rows(m), :] = jnp.dot(
                context[...], wo[:, cols(peers[k])], preferred_element_type=F32
            ).astype(BF16)
            if k:
                piece_copy(m, k).start()

    def finish(m):
        for k in range(1, n_obs):
            remote(
                pbuf.at[peers[k], rows(m), :], rbuf.at[peers[k], rows(m), :],
                r_send.at[m, k], r_recv.at[m, peers[k]], p, peers[k], z,
            ).wait_recv()
        head_total = pbuf[o, rows(m), :].astype(F32)
        for k in range(1, n_obs):
            head_total = head_total + rbuf[peers[k], rows(m), :].astype(F32)
        result = (xbuf[rows(m), cols(o)].astype(F32) + head_total).astype(BF16)
        out[rows(m), :] = result

        @pl.when(p == 0)
        def _():
            x1[rows(m), :] = result
            for k in range(n_obs):
                x1_copy(m, (k + 1) % n_obs).start()

    @pl.loop(0, micro + 1)
    def _(t):
        @pl.when(t < micro)
        def _():
            @pl.when(p == 1)
            def _():
                remote(
                    x1.at[rows(t), :], xbuf.at[rows(t), cols(o)],
                    x_send.at[t, 0], x_recv.at[t, o], 0, o, z,
                ).wait_recv()
                project(t)

            attend(t)

        @pl.when(t > 0)
        def _():
            finish(t - 1)

    for k in range(1, n_patch):
        z_copy(k).wait_send()
    for k in range(n_obs):
        sel_copy(k).wait_send()
        if k:
            forward(k).wait_send()

    @pl.loop(0, micro)
    def _(m):
        for k in range(1, n_obs):
            piece_copy(m, k).wait_send()

        @pl.when(p == 0)
        def _():
            for k in range(1, n_obs):
                patch_copy(m, k).wait_send()
            for k in range(n_obs):
                x1_copy(m, k).wait_send()


def on_device(
    n_obs,
    n_patch,
    patch_tokens,
    obs_tokens,
    footprint,
    list_counts,
    footprint_bias,
    w_query,
    w_key,
    w_value,
    w_out,
    patch_gain,
    obs_gain,
):
    row_count, feat = patch_tokens.shape
    width = feat * n_obs
    head_width = w_query.shape[2]
    range_blocks = obs_tokens.shape[0] // BLK
    micro = row_count // BLK
    half_rows = n_patch * HALF
    anywhere = pl.BlockSpec(memory_space=pl.ANY)
    vmem = pl.BlockSpec(memory_space=pltpu.VMEM)
    dma = pltpu.SemaphoreType.DMA
    result = pl.pallas_call(
        functools.partial(kernel, n_obs, n_patch),
        out_shape=jax.ShapeDtypeStruct((row_count, feat), BF16),
        in_specs=[anywhere, anywhere, vmem, vmem, vmem] + [anywhere] * 4 + [vmem, vmem],
        out_specs=vmem,
        scratch_shapes=[
            pltpu.VMEM((width, head_width), BF16),
            pltpu.VMEM((width, head_width), BF16),
            pltpu.VMEM((width, head_width), BF16),
            pltpu.VMEM((head_width, width), BF16),
            pltpu.VMEM((row_count, width), BF16),
            pltpu.VMEM((n_patch, range_blocks, HALF, feat), BF16),
            pltpu.VMEM((half_rows, feat), BF16),
            pltpu.VMEM((2, half_rows, width), BF16),
            pltpu.VMEM((2 * half_rows, head_width), BF16),
            pltpu.VMEM((2 * half_rows, head_width), BF16),
            pltpu.VMEM((row_count, head_width), BF16),
            pltpu.VMEM((BLK, head_width), BF16),
            pltpu.VMEM((n_obs, row_count, feat), BF16),
            pltpu.VMEM((n_obs, row_count, feat), BF16),
            pltpu.VMEM((row_count, feat), BF16),
            pltpu.VMEM((micro, 2 * half_rows), F32),
            dma((4,)),
            dma((3,)),
            dma((n_patch,)),
            dma((n_patch,)),
            dma((n_obs,)),
            dma((2, n_obs)),
            dma((n_obs,)),
            dma((2 * micro, n_obs)),
            dma((micro, n_obs)),
            dma((micro, n_obs)),
            dma((micro, n_obs)),
        ],
        compiler_params=pltpu.CompilerParams(
            collective_id=0, has_side_effects=True, vmem_limit_bytes=44 * 1024 * 1024
        ),
    )(
        patch_tokens,
        obs_tokens.reshape(range_blocks, 2, HALF, feat),
        footprint,
        list_counts[:, None],
        footprint_bias,
        w_query[0],
        w_key[0],
        w_value[0],
        w_out[0],
        patch_gain,
        obs_gain,
    )
    return result[None]


def solution(mesh):
    in_specs = (
        P("patch", "obs"),
        P("patch", "obs"),
        P("patch", None),
        P("patch"),
        P("patch", None),
        P("pipe", None, "obs"),
        P("pipe", None, "obs"),
        P("pipe", None, "obs"),
        P("pipe", "obs", None),
        P("pipe", None),
        P("pipe", None),
    )
    out_specs = P("pipe", "patch", "obs")
    return jax.shard_map(
        functools.partial(on_device, mesh.shape["obs"], mesh.shape["patch"]),
        mesh=mesh, in_specs=in_specs, out_specs=out_specs, check_vma=False,
    )
```

time: 474 us -> 87 us (0.18)
  waiting for transfers between devices: 354 us -> 0 us
  Pallas kernels: 0 us -> 73.9 us
  matrix products: 37.5 us -> 0 us
  local copies, waits for them, and re-layouts: 36.6 us -> 12.6 us
  other arithmetic: 23.9 us -> 0 us
  between operations: 13.9 us -> 0.02 us
  starting transfers between devices: 5.63 us -> 0 us
    psum x5 -> x0, waiting for transfers between devices: 236 us -> none  [on_device(): lax.psum(partial_value.astype(jnp.bfloat16), 'obs').astype(jnp.float32)]
    all_gather x3 -> x0, waiting for transfers between devices: 107 us -> none  [the longest x1 45.6 us: on_device(): kv_table = lax.all_gather(local_blocks, 'patch', axis=0, tiled=True)]
    pallas_call x0 -> x1, Pallas kernels: none -> 73.9 us  [on_device(): pl.pallas_call(functools.partial(kernel, n_obs, n_patch), out_shape=jax.S...]
    dot_general x18 -> x0, matrix products: 35.6 us -> none  [the longest x4 11 us: attend_block(): jnp.einsum('bhqk,bkhd->bqhd', weights, value_part, preferred_element_type...]
    gather x4 -> x0, local copies, waits for them, and re-layouts: 11.7 us -> none  [attend_block(): kv_table[slot_part].reshape(blocks_micro, list_slots * BLK, 2 * head_width)]
    ppermute x4 -> x0, waiting for transfers between devices: 10.2 us -> none  [passed_along(): lax.ppermute(value, axis, [(source, source + steps) for source in range(f...]
    cond x12 -> x0, local copies, waits for them, and re-layouts: 10.2 us -> none
    select_n x5 -> x0, other arithmetic: 7.75 us -> none  [on_device(): segment_input = jnp.where(pipe_segment == 0, own_rows, arriving)]
  transfers between devices with their start and end apart: 12 -> 0, of which waited for: 12 -> 0; matrix products, arithmetic and copies ran while one was open for 2% -> 0% of each run, Pallas kernels for 0% -> 0%
where the time goes in v1:
time: 87 us; the launch traced here: 86.6 us
  Pallas kernels  73.9 us (85%)
  local copies, waits for them, and re-layouts  12.6 us (14%)
    pallas_call x1, Pallas kernels, on_device(): pl.pallas_call(functools.partial(kernel, n_obs, n_patch), out_shape=jax.S...  73.9 us
    unnamed x21, local copies, waits for them, and re-layouts  11.9 us

profile of v1, /device:TPU:1, one launch (start us, length us, event | category | flops | bytes accessed | tf_op | source)
XLA Modules:
  0.0 86.6 jit_solution(12132217455894985491)
XLA Ops:
  0.0 0.7 copy.12.counts
  0.7 0.0 copy-start
  0.7 1.6 %copy-done = bf16[1,2048,512]{2,1,0:T(8,128)(2,1)S(1)} copy-done((bf16[1,2048,512]{2,1,0:T(8,128)(2,1)S(1)}, bf16[1,2048,512]{2,1,0:T(8,128)(2,1)}, u32[]{:S(2)}) %copy-start) | copy-done | bytes 2097176
  2.3 0.0 copy-start.1
  2.3 1.6 %copy-done.1 = bf16[1,2048,512]{2,1,0:T(8,128)(2,1)S(1)} copy-done((bf16[1,2048,512]{2,1,0:T(8,128)(2,1)S(1)}, bf16[1,2048,512]{2,1,0:T(8,128)(2,1)}, u32[]{:S(2)}) %copy-start.1) | copy-done | bytes 2097176
  3.9 0.0 copy-start.2
  3.9 1.6 %copy-done.2 = bf16[1,2048,512]{2,1,0:T(8,128)(2,1)S(1)} copy-done((bf16[1,2048,512]{2,1,0:T(8,128)(2,1)S(1)}, bf16[1,2048,512]{2,1,0:T(8,128)(2,1)}, u32[]{:S(2)}) %copy-start.2) | copy-done | bytes 2097176
  5.5 0.0 copy-start.3
  5.5 1.6 %copy-done.3 = bf16[1,512,2048]{2,1,0:T(8,128)(2,1)S(1)} copy-done((bf16[1,512,2048]{2,1,0:T(8,128)(2,1)S(1)}, bf16[1,512,2048]{2,1,0:T(8,128)(2,1)}, u32[]{:S(2)}) %copy-start.3) | copy-done | bytes 2097176
  7.1 0.0 copy-start.4
  7.1 1.0 %copy-done.4 = bf16[512,512]{1,0:T(8,128)(2,1)S(1)} copy-done((bf16[512,512]{1,0:T(8,128)(2,1)S(1)}, bf16[512,512]{1,0:T(8,128)(2,1)}, u32[]{:S(2)}) %copy-start.4) | copy-done | bytes 524312
  8.2 0.0 copy-start.5
  8.2 0.9 %copy-done.5 = bf16[256,512]{1,0:T(8,128)(2,1)S(1)} copy-done((bf16[256,512]{1,0:T(8,128)(2,1)S(1)}, bf16[256,512]{1,0:T(8,128)(2,1)}, u32[]{:S(2)}) %copy-start.5) | copy-done | bytes 262168
  9.1 0.0 copy-start.6
  9.1 0.7 copy-done.6
  9.8 0.0 copy-start.7
  9.8 0.7 copy-done.7
  10.5 0.0 copy-start.8
  10.5 0.7 copy-done.8
  11.2 0.0 copy-start.9
  11.2 0.7 copy-done.9
  11.9 73.9 %shard_map.109 = bf16[512,512]{1,0:T(8,128)(2,1)S(1)} custom-call(bf16[512,512]{1,0:T(8,128)(2,1)S(1)} %copy-done.4, bf16[2,2,64,512]{3,2,1,0:T(8,128)(2,1)S(1)} %bitcast.12, s32[4,4]{1,0:T(4,128)S(1)} %copy-done.8, s32[4,1]{1,0:T(4,128)S(1)} %copy.12.counts, f32[4,4]{1,0:T(4,128)S(1)} %copy-done.9, bf16[2048,512]{1,0:T(8,128)(2,1)S(1)} %bitcast.7, ...), custom_call_target="tpu_custom_call" | custom-call | tf_op jit(solution)/shard_map/pallas_call | solution.py:358
  85.8 0.8 copy.14
Async XLA Ops:
  0.7 1.6 %copy-start = (bf16[1,2048,512]{2,1,0:T(8,128)(2,1)S(1)}, bf16[1,2048,512]{2,1,0:T(8,128)(2,1)}, u32[]{:S(2)}) copy-start(bf16[1,2048,512]{2,1,0:T(8,128)(2,1)} %param.16) | copy-start | bytes 6291460
  2.3 1.6 %copy-start.1 = (bf16[1,2048,512]{2,1,0:T(8,128)(2,1)S(1)}, bf16[1,2048,512]{2,1,0:T(8,128)(2,1)}, u32[]{:S(2)}) copy-start(bf16[1,2048,512]{2,1,0:T(8,128)(2,1)} %param.17) | copy-start | bytes 6291460
  3.9 1.6 %copy-start.2 = (bf16[1,2048,512]{2,1,0:T(8,128)(2,1)S(1)}, bf16[1,2048,512]{2,1,0:T(8,128)(2,1)}, u32[]{:S(2)}) copy-start(bf16[1,2048,512]{2,1,0:T(8,128)(2,1)} %param.18) | copy-start | bytes 6291460
  5.5 1.6 %copy-start.3 = (bf16[1,512,2048]{2,1,0:T(8,128)(2,1)S(1)}, bf16[1,512,2048]{2,1,0:T(8,128)(2,1)}, u32[]{:S(2)}) copy-start(bf16[1,512,2048]{2,1,0:T(8,128)(2,1)} %param.19) | copy-start | bytes 6291460
  7.1 1.0 %copy-start.4 = (bf16[512,512]{1,0:T(8,128)(2,1)S(1)}, bf16[512,512]{1,0:T(8,128)(2,1)}, u32[]{:S(2)}) copy-start(bf16[512,512]{1,0:T(8,128)(2,1)} %patch_hbm.1) | copy-start | bytes 1572868
  8.2 0.9 %copy-start.5 = (bf16[256,512]{1,0:T(8,128)(2,1)S(1)}, bf16[256,512]{1,0:T(8,128)(2,1)}, u32[]{:S(2)}) copy-start(bf16[256,512]{1,0:T(8,128)(2,1)} %param.12) | copy-start | bytes 786436
  9.1 0.7 copy-start.6
  9.8 0.7 copy-start.7
  10.5 0.7 copy-start.8
  11.2 0.7 copy-start.9

commit v2 on v1

--- a/solution.py
+++ b/solution.py
@@ -37,22 +37,29 @@
     n_patch,
     patch_hbm,
     obs_hbm,
-    footprint,
+    footprint_hbm,
     counts,
-    slot_bias,
+    slot_bias_hbm,
     wq_hbm,
     wk_hbm,
     wv_hbm,
     wo_hbm,
+    patch_gain_hbm,
+    obs_gain_hbm,
+    out,
+    footprint,
+    slot_bias,
     patch_gain,
     obs_gain,
-    out,
     wq,
     wk,
     wv,
     wo,
     xbuf,
-    zbuf,
+    obs_own,
+    zout,
+    wish,
+    asked,
     sel,
     ofull,
     keys,
@@ -65,6 +72,8 @@
     bias,
     w_sem,
     own_sem,
+    a_send,
+    a_recv,
     z_send,
     z_recv,
     o_send,
@@ -81,7 +90,7 @@
     rows_total, feat = out.shape
     micro = rows_total // BLK
     heads = wq.shape[1] // HS
-    range_blocks = zbuf.shape[1]
+    range_blocks = obs_own.shape[0]
     half_rows = sel.shape[0]
     peers = [lax.rem(o + k, n_obs) for k in range(n_obs)]
     zpeers = [lax.rem(z + k, n_patch) for k in range(n_patch)]
@@ -108,7 +117,20 @@
             barrier, inc=1, device_id={"pipe": p, "obs": o, "patch": zpeers[k]},
             device_id_type=pl.DeviceIdType.MESH,
         )
-    own_obs = pltpu.make_async_copy(obs_hbm.at[:, p], zbuf.at[z], own_sem.at[0])
+    small_copies = [
+        pltpu.make_async_copy(src, dst, w_sem.at[4 + i])
+        for i, (src, dst) in enumerate(
+            (
+                (footprint_hbm, footprint),
+                (slot_bias_hbm, slot_bias),
+                (patch_gain_hbm, patch_gain),
+                (obs_gain_hbm, obs_gain),
+            )
+        )
+    ]
+    for copy in small_copies:
+        copy.start()
+    own_obs = pltpu.make_async_copy(obs_hbm.at[:, p], obs_own, own_sem.at[0])
     own_obs.start()
     own_patch = pltpu.make_async_copy(patch_hbm, xbuf.at[:, cols(o)], own_sem.at[1])
 
@@ -124,58 +146,81 @@
     ]
     for copy in w_copies:
         copy.start()
-    pl.semaphore_wait(barrier, 2 * n_obs - 1 + n_patch - 1)
-
-    def z_copy(k):
-        return remote(
-            obs_hbm.at[:, p], zbuf.at[z], z_send.at[k], z_recv.at[z], p, o, zpeers[k]
-        )
-
-    def patch_copy(m, k):
-        return remote(
-            patch_hbm.at[rows(m), :], xbuf.at[rows(m), cols(o)],
-            x_send.at[m, k], x_recv.at[m, o], 0, peers[k], z,
-        )
-
-    for k in range(1, n_patch):
-        z_copy(k).start()
-
-    @pl.when(p == 0)
-    def _():
-        @pl.loop(0, micro)
-        def _(m):
-            for k in range(1, n_obs):
-                patch_copy(m, k).start()
-
+    small_copies[0].wait()
+    small_copies[1].wait()
     listed = footprint[...].astype(F32)
     slots = lax.broadcasted_iota(jnp.int32, listed.shape, 1)
-    alive = slots < counts[...]
+    row = lax.broadcasted_iota(jnp.int32, listed.shape, 0)
+    live = jnp.zeros(listed.shape, jnp.int32)
+    for b in range(listed.shape[0]):
+        live = jnp.where(row == b, counts[b], live)
+    alive = slots < live
     added = slot_bias[...]
     col = lax.broadcasted_iota(jnp.int32, bias.shape, 1)
     source = lax.rem(lax.div(col, HALF), n_patch)
     full_bias = jnp.full(bias.shape, NEG, F32)
-    wanted = []
     for zz in range(n_patch):
         low = zz * range_blocks
         match = alive & (listed >= float(low)) & (listed < float(low + range_blocks))
         one = jnp.max(jnp.where(match, added, NEG), axis=1, keepdims=True)
         full_bias = jnp.where(source == zz, one, full_bias)
         which = jnp.max(jnp.where(match, listed - float(low), 0.0), axis=1, keepdims=True)
-        wanted.append(jnp.max(which, axis=0, keepdims=True))
+        wish[zz] = jnp.broadcast_to(jnp.max(which, axis=0, keepdims=True), wish.shape[1:])
     bias[...] = full_bias
 
+    pl.semaphore_wait(barrier, 2 * n_obs - 1 + n_patch - 1)
+
+    def wish_copy(k):
+        return remote(
+            wish.at[zpeers[k]], asked.at[z], a_send.at[k], a_recv.at[z], p, o, zpeers[k]
+        )
+
+    def z_place(index):
+        return pl.ds(pl.multiple_of(index * HALF, HALF), HALF)
+
+    def z_copy(k):
+        return remote(
+            zout.at[k], sel.at[z_place(z), :], z_send.at[k], z_recv.at[z], p, o, zpeers[k]
+        )
+
+    def patch_copy(m, k):
+        return remote(
+            patch_hbm.at[rows(m), :], xbuf.at[rows(m), cols(o)],
+            x_send.at[m, k], x_recv.at[m, o], 0, peers[k], z,
+        )
+
+    def pick(which):
+        which = jnp.broadcast_to(which[0:1, 0:1], obs_own.shape[1:])
+        picked = obs_own[0].astype(F32)
+        for k in range(1, range_blocks):
+            picked = jnp.where(which == float(k), obs_own[k].astype(F32), picked)
+        return picked.astype(BF16)
+
+    early = micro - 1
+    for k in range(1, n_patch):
+        wish_copy(k).start()
+
+    @pl.when(p == 0)
+    def _():
+        @pl.loop(0, early)
+        def _(m):
+            for k in range(1, n_obs):
+                patch_copy(m, k).start()
+
     own_obs.wait()
+    sel[z_place(z), :] = pick(wish[z])
     for k in range(1, n_patch):
         remote(
-            obs_hbm.at[:, p], zbuf.at[zpeers[k]], z_send.at[k], z_recv.at[zpeers[k]],
+            wish.at[zpeers[k]], asked.at[zpeers[k]], a_send.at[k], a_recv.at[zpeers[k]],
             p, o, zpeers[k],
         ).wait_recv()
-    for zz in range(n_patch):
-        picked = zbuf[zz, 0].astype(F32)
-        which = jnp.broadcast_to(wanted[zz], picked.shape)
-        for k in range(1, range_blocks):
-            picked = jnp.where(which == float(k), zbuf[zz, k].astype(F32), picked)
-        sel[zz * HALF : (zz + 1) * HALF, :] = picked.astype(BF16)
+        zout[k] = pick(asked[zpeers[k]])
+        z_copy(k).start()
+    for k in range(1, n_patch):
+        remote(
+            zout.at[k], sel.at[z_place(zpeers[k]), :], z_send.at[k], z_recv.at[zpeers[k]],
+            p, o, zpeers[k],
+        ).wait_recv()
 
     def sel_copy(k):
         if k == 0:
@@ -198,7 +243,17 @@
     own_sel = pltpu.make_async_copy(sel, ofull.at[p, :, cols(o)], own_sem.at[2])
     own_sel.start()
 
+    @pl.when(p == 0)
+    def _():
+        @pl.loop(early, micro)
+        def _(m):
+            for k in range(1, n_obs):
+                patch_copy(m, k).start()
+
+
     w_copies[0].wait()
+    small_copies[2].wait()
+    small_copies[3].wait()
     score_scale = HS ** (-0.5)
 
     def project(m):
@@ -216,7 +271,7 @@
     def _():
         own_patch.wait()
 
-        @pl.loop(0, micro)
+        @pl.loop(0, early)
         def _(m):
             project(m)
 
@@ -303,6 +358,9 @@
                     x1.at[rows(t), :], xbuf.at[rows(t), cols(o)],
                     x_send.at[t, 0], x_recv.at[t, o], 0, o, z,
                 ).wait_recv()
+
+            @pl.when((p == 1) | (t >= early))
+            def _():
                 project(t)
 
             attend(t)
@@ -312,6 +370,7 @@
             finish(t - 1)
 
     for k in range(1, n_patch):
+        wish_copy(k).wait_send()
         z_copy(k).wait_send()
     for k in range(n_obs):
         sel_copy(k).wait_send()
@@ -352,21 +411,28 @@
     range_blocks = obs_tokens.shape[0] // BLK
     micro = row_count // BLK
     half_rows = n_patch * HALF
-    anywhere = pl.BlockSpec(memory_space=pl.ANY)
+    hbm = pl.BlockSpec(memory_space=pltpu.MemorySpace.HBM)
     vmem = pl.BlockSpec(memory_space=pltpu.VMEM)
     dma = pltpu.SemaphoreType.DMA
     result = pl.pallas_call(
         functools.partial(kernel, n_obs, n_patch),
         out_shape=jax.ShapeDtypeStruct((row_count, feat), BF16),
-        in_specs=[anywhere, anywhere, vmem, vmem, vmem] + [anywhere] * 4 + [vmem, vmem],
+        in_specs=[hbm, hbm, hbm, pl.BlockSpec(memory_space=pltpu.SMEM)] + [hbm] * 7,
         out_specs=vmem,
         scratch_shapes=[
+            pltpu.VMEM(footprint.shape, jnp.int32),
+            pltpu.VMEM(footprint_bias.shape, F32),
+            pltpu.VMEM((1, width), F32),
+            pltpu.VMEM((1, width), F32),
             pltpu.VMEM((width, head_width), BF16),
             pltpu.VMEM((width, head_width), BF16),
             pltpu.VMEM((width, head_width), BF16),
             pltpu.VMEM((head_width, width), BF16),
             pltpu.VMEM((row_count, width), BF16),
-            pltpu.VMEM((n_patch, range_blocks, HALF, feat), BF16),
+            pltpu.VMEM((range_blocks, HALF, feat), BF16),
+            pltpu.VMEM((n_patch, HALF, feat), BF16),
+            pltpu.VMEM((n_patch, 8, 128), F32),
+            pltpu.VMEM((n_patch, 8, 128), F32),
             pltpu.VMEM((half_rows, feat), BF16),
             pltpu.VMEM((2, half_rows, width), BF16),
             pltpu.VMEM((2 * half_rows, head_width), BF16),
@@ -377,8 +443,10 @@
             pltpu.VMEM((n_obs, row_count, feat), BF16),
             pltpu.VMEM((row_count, feat), BF16),
             pltpu.VMEM((micro, 2 * half_rows), F32),
-            dma((4,)),
+            dma((8,)),
             dma((3,)),
+            dma((n_patch,)),
+            dma((n_patch,)),
             dma((n_patch,)),
             dma((n_patch,)),
             dma((n_obs,)),
@@ -390,13 +458,13 @@
             dma((micro, n_obs)),
         ],
         compiler_params=pltpu.CompilerParams(
-            collective_id=0, has_side_effects=True, vmem_limit_bytes=44 * 1024 * 1024
+            collective_id=0, has_side_effects=True, vmem_limit_bytes=62 * 1024 * 1024
         ),
     )(
         patch_tokens,
         obs_tokens.reshape(range_blocks, 2, HALF, feat),
         footprint,
-        list_counts[:, None],
+        list_counts,
         footprint_bias,
         w_query[0],
         w_key[0],

time: 87 us -> 75.5 us (0.87)
  local copies, waits for them, and re-layouts: 12.6 us -> 1.87 us
    unnamed x21 -> x1, local copies, waits for them, and re-layouts: 11.9 us -> 1.87 us
where the time goes in v2:
time: 75.5 us; the launch traced here: 75.4 us
  Pallas kernels  73.5 us (97%)
  local copies, waits for them, and re-layouts  1.87 us (2%)
    pallas_call x1, Pallas kernels, on_device(): pl.pallas_call(functools.partial(kernel, n_obs, n_patch), out_shape=jax.S...  73.5 us
    unnamed x1, local copies, waits for them, and re-layouts  1.87 us

profile of v2, /device:TPU:1, one launch (start us, length us, event | category | flops | bytes accessed | tf_op | source)
XLA Modules:
  0.0 75.4 jit_solution(14672728137345152504)
XLA Ops:
  0.0 73.5 %shard_map.109 = bf16[512,512]{1,0:T(8,128)(2,1)} custom-call(bf16[512,512]{1,0:T(8,128)(2,1)} %patch_hbm.1, bf16[2,2,64,512]{3,2,1,0:T(8,128)(2,1)} %bitcast.11, s32[4,4]{1,0:T(4,128)} %footprint_hbm.1, s32[4]{0:T(128)} %counts.1, f32[4,4]{1,0:T(4,128)} %slot_bias_hbm.1, bf16[2048,512]{1,0:T(8,128)(2,1)} %bitcast.7, bf16[2048,512]{1,0:T(8,128)(2,1)} %bitcast.8, ...), custom_call_target="tpu_custom_call" | custom-call | tf_op jit(solution)/shard_map/pallas_call | solution.py:417
  73.5 1.9 %copy.13 = bf16[1,512,512]{2,1,0:T(8,128)(2,1)} copy(bf16[1,512,512]{2,1,0:T(8,128)(2,1)} %bitcast.6) | data formatting | bytes 1048576

commit v3 on v2

--- a/solution.py
+++ b/solution.py
@@ -83,6 +83,10 @@
     x_recv,
     r_send,
     r_recv,
+    xd_send,
+    xd_recv,
+    od_send,
+    od_recv,
 ):
     p = lax.axis_index("pipe")
     o = lax.axis_index("obs")
@@ -92,7 +96,14 @@
     heads = wq.shape[1] // HS
     range_blocks = obs_own.shape[0]
     half_rows = sel.shape[0]
-    peers = [lax.rem(o + k, n_obs) for k in range(n_obs)]
+    relay = n_obs == 4
+    if relay:
+        side = o + 1 - 2 * lax.rem(o, 2)
+        peers = [o, side, lax.rem(o + 2, 4), lax.rem(side + 2, 4)]
+        direct = [1, 2]
+    else:
+        peers = [lax.rem(o + k, n_obs) for k in range(n_obs)]
+        direct = list(range(1, n_obs))
     zpeers = [lax.rem(z + k, n_patch) for k in range(n_patch)]
 
     def cols(index):
@@ -204,7 +215,7 @@
     def _():
         @pl.loop(0, early)
         def _(m):
-            for k in range(1, n_obs):
+            for k in direct:
                 patch_copy(m, k).start()
 
     own_obs.wait()
@@ -237,7 +248,7 @@
             slab, slab, f_send.at[k], o_recv.at[p, peers[k]], 1 - p, o, z
         )
 
-    for k in range(1, n_obs):
+    for k in direct:
         sel_copy(k).start()
     sel_copy(0).start()
     own_sel = pltpu.make_async_copy(sel, ofull.at[p, :, cols(o)], own_sem.at[2])
@@ -247,7 +258,7 @@
     def _():
         @pl.loop(early, micro)
         def _(m):
-            for k in range(1, n_obs):
+            for k in direct:
                 patch_copy(m, k).start()
 
 
@@ -256,12 +267,37 @@
     small_copies[3].wait()
     score_scale = HS ** (-0.5)
 
+    def half_slab(m, k, column):
+        start = pl.multiple_of(m * BLK + (k - 1) * HALF, HALF)
+        return xbuf.at[pl.ds(start, HALF), cols(column)]
+
+    def pass_x(m, k):
+        slab = half_slab(m, k, peers[k])
+        return remote(
+            slab, slab, xd_send.at[m, k - 1], xd_recv.at[m, k - 1], p, peers[3 - k], z
+        )
+
+    def arrive_x(m):
+        for k in direct:
+            slab = xbuf.at[rows(m), cols(peers[k])]
+            remote(
+                slab, slab, x_send.at[m, k], x_recv.at[m, peers[k]], p, peers[k], z
+            ).wait_recv()
+            if relay:
+                pass_x(m, k).start()
+
+    def pass_o(k):
+        part = half_rows // 2
+        slab = ofull.at[p, (k - 1) * part : k * part, cols(peers[k])]
+        return remote(slab, slab, od_send.at[k - 1], od_recv.at[k - 1], p, peers[3 - k], z)
+
     def project(m):
-        for k in range(1, n_obs):
-            remote(
-                patch_hbm.at[rows(m), :], xbuf.at[rows(m), cols(peers[k])],
-                x_send.at[m, k], x_recv.at[m, peers[k]], 0, peers[k], z,
-            ).wait_recv()
+        if relay:
+            for k in direct:
+                slab = half_slab(m, k, peers[3])
+                remote(
+                    slab, slab, xd_send.at[m, k - 1], xd_recv.at[m, k - 1], p, peers[k], z
+                ).wait_recv()
         normed = rms_round(xbuf[rows(m), :], patch_gain[...])
         queries[rows(m), :] = (
             jnp.dot(normed, wq[...], preferred_element_type=F32) * score_scale
@@ -273,12 +309,41 @@
 
         @pl.loop(0, early)
         def _(m):
+            arrive_x(m)
+
+    def arrive_o():
+        for k in direct:
+            slab = ofull.at[p, :, cols(peers[k])]
+            remote(
+                sel, slab, o_send.at[k], o_recv.at[p, peers[k]], p, peers[k], z
+            ).wait_recv()
+            if relay:
+                pass_o(k).start()
+            forward(k).start()
+
+    arrive_o()
+
+    @pl.when(p == 0)
+    def _():
+        @pl.loop(0, early)
+        def _(m):
             project(m)
 
-    for k in range(1, n_obs):
-        slab = ofull.at[p, :, cols(peers[k])]
-        remote(sel, slab, o_send.at[k], o_recv.at[p, peers[k]], p, peers[k], z).wait_recv()
-        forward(k).start()
+    if relay:
+        for k in direct:
+            part = half_rows // 2
+            slab = ofull.at[p, (k - 1) * part : k * part, cols(peers[3])]
+            remote(
+                slab, slab, od_send.at[k - 1], od_recv.at[k - 1], p, peers[k], z
+            ).wait_recv()
+        forward(3).start()
+
+    @pl.when(p == 0)
+    def _():
+        @pl.loop(early, micro)
+        def _(m):
+            arrive_x(m)
+
     own_sel.wait()
     for k in range(n_obs):
         slab = ofull.at[1 - p, :, cols(peers[k])]
@@ -323,7 +388,7 @@
             total = jnp.sum(weights, axis=-1, keepdims=True)
             mixed = jnp.dot(weights.astype(BF16), vals[:, head], preferred_element_type=F32)
             context[:, head] = (mixed / total).astype(BF16)
-        for k in list(range(1, n_obs)) + [0]:
+        for k in list(range(n_obs - 1, 0, -1)) + [0]:
             pbuf[peers[k], rows(m), :] = jnp.dot(
                 context[...], wo[:, cols(peers[k])], preferred_element_type=F32
             ).astype(BF16)
@@ -345,8 +410,8 @@
         @pl.when(p == 0)
         def _():
             x1[rows(m), :] = result
-            for k in range(n_obs):
-                x1_copy(m, (k + 1) % n_obs).start()
+            for k in direct + [0]:
+                x1_copy(m, k).start()
 
     @pl.loop(0, micro + 1)
     def _(t):
@@ -358,6 +423,7 @@
                     x1.at[rows(t), :], xbuf.at[rows(t), cols(o)],
                     x_send.at[t, 0], x_recv.at[t, o], 0, o, z,
                 ).wait_recv()
+                arrive_x(t)
 
             @pl.when((p == 1) | (t >= early))
             def _():
@@ -372,21 +438,27 @@
     for k in range(1, n_patch):
         wish_copy(k).wait_send()
         z_copy(k).wait_send()
-    for k in range(n_obs):
+    for k in [0] + direct:
         sel_copy(k).wait_send()
-        if k:
-            forward(k).wait_send()
+    for k in range(1, n_obs):
+        forward(k).wait_send()
+    if relay:
+        for k in direct:
+            pass_o(k).wait_send()
 
     @pl.loop(0, micro)
     def _(m):
         for k in range(1, n_obs):
             piece_copy(m, k).wait_send()
+        if relay:
+            for k in direct:
+                pass_x(m, k).wait_send()
 
         @pl.when(p == 0)
         def _():
-            for k in range(1, n_obs):
+            for k in direct:
                 patch_copy(m, k).wait_send()
-            for k in range(n_obs):
+            for k in [0] + direct:
                 x1_copy(m, k).wait_send()
 
 
@@ -456,6 +528,10 @@
             dma((micro, n_obs)),
             dma((micro, n_obs)),
             dma((micro, n_obs)),
+            dma((micro, 2)),
+            dma((micro, 2)),
+            dma((2,)),
+            dma((2,)),
         ],
         compiler_params=pltpu.CompilerParams(
             collective_id=0, has_side_effects=True, vmem_limit_bytes=62 * 1024 * 1024

time: 75.5 us -> 82 us (1.086)
  Pallas kernels: 73.5 us -> 79.9 us
    pallas_call x1, Pallas kernels: 73.5 us -> 79.9 us  [on_device(): pl.pallas_call(functools.partial(kernel, n_obs, n_patch), out_shape=jax.S...]
where the time goes in v3:
time: 82 us; the launch traced here: 81.8 us
  Pallas kernels  79.9 us (97%)
  local copies, waits for them, and re-layouts  1.87 us (2%)
    pallas_call x1, Pallas kernels, on_device(): pl.pallas_call(functools.partial(kernel, n_obs, n_patch), out_shape=jax.S...  79.9 us
    unnamed x1, local copies, waits for them, and re-layouts  1.87 us

profile of v3, /device:TPU:1, one launch (start us, length us, event | category | flops | bytes accessed | tf_op | source)
XLA Modules:
  0.0 81.8 jit_solution(6558116116109758811)
XLA Ops:
  0.0 79.9 %shard_map.109 = bf16[512,512]{1,0:T(8,128)(2,1)} custom-call(bf16[512,512]{1,0:T(8,128)(2,1)} %patch_hbm.1, bf16[2,2,64,512]{3,2,1,0:T(8,128)(2,1)} %bitcast.11, s32[4,4]{1,0:T(4,128)} %footprint_hbm.1, s32[4]{0:T(128)} %counts.1, f32[4,4]{1,0:T(4,128)} %slot_bias_hbm.1, bf16[2048,512]{1,0:T(8,128)(2,1)} %bitcast.7, bf16[2048,512]{1,0:T(8,128)(2,1)} %bitcast.8, ...), custom_call_target="tpu_custom_call" | custom-call | tf_op jit(solution)/shard_map/pallas_call | solution.py:489
  79.9 1.9 %copy.13 = bf16[1,512,512]{2,1,0:T(8,128)(2,1)} copy(bf16[1,512,512]{2,1,0:T(8,128)(2,1)} %bitcast.6) | data formatting | bytes 1048576

commit v4 on v3

--- a/solution.py
+++ b/solution.py
@@ -291,13 +291,15 @@
         slab = ofull.at[p, (k - 1) * part : k * part, cols(peers[k])]
         return remote(slab, slab, od_send.at[k - 1], od_recv.at[k - 1], p, peers[3 - k], z)
 
-    def project(m):
+    def arrive_diagonal(m):
         if relay:
             for k in direct:
                 slab = half_slab(m, k, peers[3])
                 remote(
                     slab, slab, xd_send.at[m, k - 1], xd_recv.at[m, k - 1], p, peers[k], z
                 ).wait_recv()
+
+    def project(m):
         normed = rms_round(xbuf[rows(m), :], patch_gain[...])
         queries[rows(m), :] = (
             jnp.dot(normed, wq[...], preferred_element_type=F32) * score_scale
@@ -327,6 +329,7 @@
     def _():
         @pl.loop(0, early)
         def _(m):
+            arrive_diagonal(m)
             project(m)
 
     if relay:
@@ -410,7 +413,7 @@
         @pl.when(p == 0)
         def _():
             x1[rows(m), :] = result
-            for k in direct + [0]:
+            for k in list(range(n_obs - 1, 0, -1)) + [0]:
                 x1_copy(m, k).start()
 
     @pl.loop(0, micro + 1)
@@ -423,7 +426,15 @@
                     x1.at[rows(t), :], xbuf.at[rows(t), cols(o)],
                     x_send.at[t, 0], x_recv.at[t, o], 0, o, z,
                 ).wait_recv()
-                arrive_x(t)
+                for k in range(1, n_obs):
+                    slab = xbuf.at[rows(t), cols(peers[k])]
+                    remote(
+                        slab, slab, x_send.at[t, k], x_recv.at[t, peers[k]], p, peers[k], z
+                    ).wait_recv()
+
+            @pl.when((p == 0) & (t >= early))
+            def _():
+                arrive_diagonal(t)
 
             @pl.when((p == 1) | (t >= early))
             def _():
@@ -450,15 +461,15 @@
     def _(m):
         for k in range(1, n_obs):
             piece_copy(m, k).wait_send()
-        if relay:
-            for k in direct:
-                pass_x(m, k).wait_send()
 
         @pl.when(p == 0)
         def _():
+            if relay:
+                for k in direct:
+                    pass_x(m, k).wait_send()
             for k in direct:
                 patch_copy(m, k).wait_send()
-            for k in [0] + direct:
+            for k in range(n_obs):
                 x1_copy(m, k).wait_send()
 
 

time: 82 us -> 74.3 us (0.906)
  Pallas kernels: 79.9 us -> 72.2 us
    pallas_call x1, Pallas kernels: 79.9 us -> 72.2 us  [on_device(): pl.pallas_call(functools.partial(kernel, n_obs, n_patch), out_shape=jax.S...]
where the time goes in v4:
time: 74.3 us; the launch traced here: 74.1 us
  Pallas kernels  72.2 us (97%)
  local copies, waits for them, and re-layouts  1.87 us (3%)
    pallas_call x1, Pallas kernels, on_device(): pl.pallas_call(functools.partial(kernel, n_obs, n_patch), out_shape=jax.S...  72.2 us
    unnamed x1, local copies, waits for them, and re-layouts  1.87 us

profile of v4, /device:TPU:1, one launch (start us, length us, event | category | flops | bytes accessed | tf_op | source)
XLA Modules:
  0.0 74.1 jit_solution(6694786497406780559)
XLA Ops:
  0.0 72.2 %shard_map.109 = bf16[512,512]{1,0:T(8,128)(2,1)} custom-call(bf16[512,512]{1,0:T(8,128)(2,1)} %patch_hbm.1, bf16[2,2,64,512]{3,2,1,0:T(8,128)(2,1)} %bitcast.11, s32[4,4]{1,0:T(4,128)} %footprint_hbm.1, s32[4]{0:T(128)} %counts.1, f32[4,4]{1,0:T(4,128)} %slot_bias_hbm.1, bf16[2048,512]{1,0:T(8,128)(2,1)} %bitcast.7, bf16[2048,512]{1,0:T(8,128)(2,1)} %bitcast.8, ...), custom_call_target="tpu_custom_call" | custom-call | tf_op jit(solution)/shard_map/pallas_call | solution.py:500
  72.2 1.9 %copy.13 = bf16[1,512,512]{2,1,0:T(8,128)(2,1)} copy(bf16[1,512,512]{2,1,0:T(8,128)(2,1)} %bitcast.6) | data formatting | bytes 1048576
